TPU v7x, 32 devices: a whole 2x2x4 slice. The times are simulated.
32 devices in a mesh: seq: 8 (over y, x, core), chan: 4 (over z).
Axes of the slice: x: 2, y: 2, z: 4, core: 2. Of those that a mesh axis runs over, the one named last changes fastest.
Arguments:
- layer_input: bfloat16 [1024, 4096], P('seq', 'chan'), may hold values from -6 to 6
- gate_query: bfloat16 [1024, 4096], P('seq', 'chan'), may hold values from -6 to 6
- gate_key: bfloat16 [1024, 4096], P('seq', 'chan'), may hold values from -6 to 6
- value_proj: bfloat16 [1024, 4096], P('seq', 'chan'), may hold values from -6 to 6
- grad_out: bfloat16 [1024, 4096], P('seq', 'chan'), may hold values from -6 to 6
- filter_taps: bfloat16 [1024, 4096], P('seq', 'chan'), may hold values from -1.1 to 1.1
Outputs:
- grad_query: bfloat16 [1024, 4096], P('seq', 'chan')
- grad_key: bfloat16 [1024, 4096], P('seq', 'chan')
- grad_value: bfloat16 [1024, 4096], P('seq', 'chan')
- grad_filter: bfloat16 [1024, 4096], P('seq', 'chan')
- grad_weight: float32 [4096, 4096], P('seq', 'chan')
All inputs are finite; a program needn't handle non-finite values.
Results may differ from a plain program's by a relative error of at most 0.0067.
Values may be sent and summed in bfloat16 or wider, within the bound.
A program may use at most 128 MiB of HBM per device.

v0:
```python
import math

import jax
import jax.numpy as jnp
from jax import lax
from jax.sharding import PartitionSpec as P

FULL_PRECISION = lax.Precision.HIGHEST


def angle_table(first, second, period):
    product = first[:, None] * second[None, :] % period
    return product.astype(jnp.float32) * (2.0 * math.pi / period)


def mixed_sum(matrix, operand, form):
    return jnp.einsum(form, matrix, operand, precision=FULL_PRECISION)


def outer_forward(signal, first_cos, first_sin, twist_cos, twist_sin):
    widened = signal.astype(jnp.float32)
    real_part = mixed_sum(first_cos, widened, "ka,ajc->kjc")
    other_part = -mixed_sum(first_sin, widened, "ka,ajc->kjc")
    cosine = twist_cos[:, :, None]
    sine = twist_sin[:, :, None]
    turned_real = real_part * cosine + other_part * sine
    turned_other = other_part * cosine - real_part * sine
    return (turned_real.astype(jnp.bfloat16), turned_other.astype(jnp.bfloat16))


def inner_forward(real_in, other_in, cosine, sine):
    real_wide = real_in.astype(jnp.float32)
    other_wide = other_in.astype(jnp.float32)
    real_out = mixed_sum(cosine, real_wide, "mj,rjc->rmc") + mixed_sum(
        sine, other_wide, "mj,rjc->rmc"
    )
    other_out = mixed_sum(cosine, other_wide, "mj,rjc->rmc") - mixed_sum(
        sine, real_wide, "mj,rjc->rmc"
    )
    return (real_out, other_out)


def inner_inverse(spectrum, cosine, sine, twist_cos, twist_sin):
    real_in, other_in = spectrum
    real_mid = mixed_sum(cosine, real_in, "jm,rmc->rjc") - mixed_sum(sine, other_in, "jm,rmc->rjc")
    other_mid = mixed_sum(cosine, other_in, "jm,rmc->rjc") + mixed_sum(sine, real_in, "jm,rmc->rjc")
    turn_cos = twist_cos[:, :, None]
    turn_sin = twist_sin[:, :, None]
    real_out = real_mid * turn_cos - other_mid * turn_sin
    other_out = real_mid * turn_sin + other_mid * turn_cos
    return (real_out.astype(jnp.bfloat16), other_out.astype(jnp.bfloat16))


def outer_inverse(real_in, other_in, cosine, sine, factor):
    total = mixed_sum(cosine, real_in.astype(jnp.float32), "ak,kjc->ajc") - mixed_sum(
        sine, other_in.astype(jnp.float32), "ak,kjc->ajc"
    )
    return (total * factor).astype(jnp.bfloat16)


def spectral_products(mixed_spec, taps_spec, gated_spec):
    mixed_real, mixed_other = mixed_spec
    taps_real, taps_other = taps_spec
    gated_real, gated_other = gated_spec
    forward_pair = (
        mixed_real * taps_real - mixed_other * taps_other,
        mixed_real * taps_other + mixed_other * taps_real,
    )
    backward_pair = (
        gated_real * taps_real + gated_other * taps_other,
        gated_other * taps_real - gated_real * taps_other,
    )
    filter_pair = (
        gated_real * mixed_real + gated_other * mixed_other,
        gated_other * mixed_real - gated_real * mixed_other,
    )
    return (forward_pair, backward_pair, filter_pair)


def shards(layer_input, gate_query, gate_key, value_proj, grad_out, filter_taps):
    rows = gate_query.shape[0]
    width = gate_query.shape[1]
    half = width // 2
    blocks = lax.axis_size("seq")
    share = rows // blocks
    length = rows * blocks
    period = 2 * length
    index = lax.axis_index("seq")
    outer_count = 2 * blocks
    block_ids = jnp.arange(blocks, dtype=jnp.int32)
    freq_ids = jnp.arange(outer_count, dtype=jnp.int32)
    row_ids = jnp.arange(rows, dtype=jnp.int32)
    first_angle = angle_table(freq_ids, block_ids, outer_count)
    first_cos = jnp.cos(first_angle)
    first_sin = jnp.sin(first_angle)
    local_rows = index * share + jnp.arange(share, dtype=jnp.int32)
    twist_angle = angle_table(freq_ids, local_rows, period)
    twist_cos = jnp.cos(twist_angle)
    twist_sin = jnp.sin(twist_angle)
    inner_angle = angle_table(row_ids, row_ids, rows)
    inner_cos = jnp.cos(inner_angle)
    inner_sin = jnp.sin(inner_angle)
    held_freq = index * 2 + jnp.arange(2, dtype=jnp.int32)
    back_angle = angle_table(held_freq, row_ids, period)
    back_cos = jnp.cos(back_angle)
    back_sin = jnp.sin(back_angle)
    last_angle = angle_table(block_ids, freq_ids, outer_count)
    last_cos = jnp.cos(last_angle)
    last_sin = jnp.sin(last_angle)
    scale_root = 1.0 / math.sqrt(length)
    last_scale = 1.0 / period
    mixed = (gate_key.astype(jnp.float32) * value_proj.astype(jnp.float32)).astype(jnp.bfloat16)
    gated = (grad_out.astype(jnp.float32) * gate_query.astype(jnp.float32)).astype(jnp.bfloat16)
    features = lax.all_gather(layer_input, "chan", axis=1, tiled=True)
    conv_parts = []
    back_parts = []
    filter_parts = []
    value_parts = []
    for section in range(2):
        offset = section * half
        mixed_part = mixed[:, offset : offset + half]
        taps_part = filter_taps[:, offset : offset + half]
        gated_part = gated[:, offset : offset + half]
        spread = (
            lax.all_to_all(mixed_part[None], "seq", split_axis=1, concat_axis=0, tiled=True),
            lax.all_to_all(taps_part[None], "seq", split_axis=1, concat_axis=0, tiled=True),
            lax.all_to_all(gated_part[None], "seq", split_axis=1, concat_axis=0, tiled=True),
        )
        turned = []
        for signal in spread:
            turned.extend(outer_forward(signal, first_cos, first_sin, twist_cos, twist_sin))
        freq = (
            lax.all_to_all(turned[0], "seq", split_axis=0, concat_axis=1, tiled=True),
            lax.all_to_all(turned[1], "seq", split_axis=0, concat_axis=1, tiled=True),
            lax.all_to_all(turned[2], "seq", split_axis=0, concat_axis=1, tiled=True),
            lax.all_to_all(turned[3], "seq", split_axis=0, concat_axis=1, tiled=True),
            lax.all_to_all(turned[4], "seq", split_axis=0, concat_axis=1, tiled=True),
            lax.all_to_all(turned[5], "seq", split_axis=0, concat_axis=1, tiled=True),
        )
        mixed_spec = inner_forward(freq[0], freq[1], inner_cos, inner_sin)
        taps_spec = inner_forward(freq[2], freq[3], inner_cos, inner_sin)
        gated_spec = inner_forward(freq[4], freq[5], inner_cos, inner_sin)
        pairs = spectral_products(mixed_spec, taps_spec, gated_spec)
        rowed = []
        for spectrum in pairs:
            rowed.extend(inner_inverse(spectrum, inner_cos, inner_sin, back_cos, back_sin))
        returned = (
            lax.all_to_all(rowed[0], "seq", split_axis=1, concat_axis=0, tiled=True),
            lax.all_to_all(rowed[1], "seq", split_axis=1, concat_axis=0, tiled=True),
            lax.all_to_all(rowed[2], "seq", split_axis=1, concat_axis=0, tiled=True),
            lax.all_to_all(rowed[3], "seq", split_axis=1, concat_axis=0, tiled=True),
            lax.all_to_all(rowed[4], "seq", split_axis=1, concat_axis=0, tiled=True),
            lax.all_to_all(rowed[5], "seq", split_axis=1, concat_axis=0, tiled=True),
        )
        conv_block = outer_inverse(returned[0], returned[1], last_cos, last_sin, last_scale)
        back_block = outer_inverse(returned[2], returned[3], last_cos, last_sin, last_scale)
        filter_block = outer_inverse(
            returned[4], returned[5], last_cos, last_sin, last_scale * scale_root
        )
        restored = (
            lax.all_to_all(conv_block, "seq", split_axis=0, concat_axis=1, tiled=True),
            lax.all_to_all(back_block, "seq", split_axis=0, concat_axis=1, tiled=True),
            lax.all_to_all(filter_block, "seq", split_axis=0, concat_axis=1, tiled=True),
        )
        conv_part = restored[0][0]
        back_part = restored[1][0]
        value_part = (
            back_part.astype(jnp.float32) * gate_key[:, offset : offset + half].astype(jnp.float32)
        ).astype(jnp.bfloat16)
        conv_parts.append(conv_part)
        back_parts.append(back_part)
        filter_parts.append(restored[2][0])
        value_parts.append(value_part)
    conv_out = jnp.concatenate(conv_parts, axis=1)
    back_grad = jnp.concatenate(back_parts, axis=1)
    grad_filter = jnp.concatenate(filter_parts, axis=1)
    grad_value = jnp.concatenate(value_parts, axis=1)
    grad_query = (grad_out.astype(jnp.float32) * conv_out.astype(jnp.float32)).astype(jnp.bfloat16)
    grad_key = (back_grad.astype(jnp.float32) * value_proj.astype(jnp.float32)).astype(jnp.bfloat16)
    columns_all = lax.all_to_all(features, "seq", split_axis=1, concat_axis=0, tiled=True)
    grad_weight = (
        lax.dot_general(
            columns_all,
            lax.all_gather(grad_value, "seq", axis=0, tiled=True),
            (((0,), (0,)), ((), ())),
            preferred_element_type=jnp.float32,
        )
        * scale_root
    )
    return (grad_query, grad_key, grad_value, grad_filter, grad_weight)


def solution(mesh):
    placed = (
        P("seq", "chan"),
        P("seq", "chan"),
        P("seq", "chan"),
        P("seq", "chan"),
        P("seq", "chan"),
        P("seq", "chan"),
    )
    return jax.shard_map(
        shards,
        mesh=mesh,
        in_specs=placed,
        out_specs=(
            P("seq", "chan"),
            P("seq", "chan"),
            P("seq", "chan"),
            P("seq", "chan"),
            P("seq", "chan"),
        ),
        check_vma=False,
    )
```

profile of v0, /device:TPU:0, one launch (start us, length us, event | category | flops | bytes accessed | tf_op | source)
XLA Modules:
  0.0 460.1 jit_solution(6926864610525701008)
XLA Ops:
  11.2 5.2 %all-to-all-start.24 = ((bf16[8,2,4096]{2,1,0:T(2,128)(2,1)}), bf16[8,2,4096]{2,1,0:T(2,128)(2,1)S(1)}, u32[]{:S(2)}, u32[]{:S(2)}) async-start(bf16[8,2,4096]{2,1,0:T(2,128)(2,1)} %reshape.181), calls=%async_computation.24 | async-start | bytes 262144 | tf_op jit(solution)/shard_map/all_to_all | solution.py:127
  85.9 5.0 %all-to-all-done.25 = bf16[16,16,512]{2,1,0:T(8,128)(2,1)S(1)} async-done(((bf16[16,16,512]{2,1,0:T(8,128)(2,1)}), bf16[16,16,512]{2,1,0:T(8,128)(2,1)S(1)}, u32[]{:S(2)}, u32[]{:S(2)}) %all-to-all-start.25) | async-done | bytes 262176 | tf_op jit(solution)/shard_map/all_to_all | solution.py:137
  108.0 6.2 %all-to-all-done.13 = bf16[16,16,512]{2,1,0:T(8,128)(2,1)S(1)} async-done(((bf16[16,16,512]{2,1,0:T(8,128)(2,1)}), bf16[16,16,512]{2,1,0:T(8,128)(2,1)S(1)}, u32[]{:S(2)}, u32[]{:S(2)}) %all-to-all-start.13) | async-done | bytes 262176 | tf_op jit(solution)/shard_map/all_to_all | solution.py:135
  118.3 6.2 %all-to-all-done.14 = bf16[16,16,512]{2,1,0:T(8,128)(2,1)S(1)} async-done(((bf16[16,16,512]{2,1,0:T(8,128)(2,1)}), bf16[16,16,512]{2,1,0:T(8,128)(2,1)S(1)}, u32[]{:S(2)}, u32[]{:S(2)}) %all-to-all-start.14) | async-done | bytes 262176 | tf_op jit(solution)/shard_map/all_to_all | solution.py:136
  139.7 5.4 %all-to-all-done.11 = bf16[16,16,512]{2,1,0:T(8,128)(2,1)S(1)} async-done(((bf16[16,16,512]{2,1,0:T(8,128)(2,1)}), bf16[16,16,512]{2,1,0:T(8,128)(2,1)S(1)}, u32[]{:S(2)}, u32[]{:S(2)}) %all-to-all-start.11) | async-done | bytes 262176 | tf_op jit(solution)/shard_map/all_to_all | solution.py:134
  145.1 15.2 %all-to-all-start.5 = ((bf16[16,16,512]{2,1,0:T(8,128)(2,1)}), bf16[16,16,512]{2,1,0:T(8,128)(2,1)}, u32[]{:S(2)}, u32[]{:S(2)}) async-start(bf16[16,16,512]{2,1,0:T(8,128)(2,1)} %copy.308), calls=%async_computation.5 | async-start | bytes 524288 | tf_op jit(solution)/shard_map/all_to_all | solution.py:136
  181.3 5.3 %all-to-all-done.4 = bf16[16,16,512]{2,1,0:T(8,128)(2,1)S(1)} async-done(((bf16[16,16,512]{2,1,0:T(8,128)(2,1)}), bf16[16,16,512]{2,1,0:T(8,128)(2,1)S(1)}, u32[]{:S(2)}, u32[]{:S(2)}) %all-to-all-start.4) | async-done | bytes 262176 | tf_op jit(solution)/shard_map/all_to_all | solution.py:135
  192.1 4.8 %all-to-all-done.1 = bf16[16,16,512]{2,1,0:T(8,128)(2,1)S(1)} async-done(((bf16[16,16,512]{2,1,0:T(8,128)(2,1)}), bf16[16,16,512]{2,1,0:T(8,128)(2,1)S(1)}, u32[]{:S(2)}, u32[]{:S(2)}) %all-to-all-start.1) | async-done | bytes 262176 | tf_op jit(solution)/shard_map/all_to_all | solution.py:133
  201.8 5.4 %all-to-all-done.2 = bf16[16,16,512]{2,1,0:T(8,128)(2,1)S(1)} async-done(((bf16[16,16,512]{2,1,0:T(8,128)(2,1)}), bf16[16,16,512]{2,1,0:T(8,128)(2,1)S(1)}, u32[]{:S(2)}, u32[]{:S(2)}) %all-to-all-start.2) | async-done | bytes 262176 | tf_op jit(solution)/shard_map/all_to_all | solution.py:134
  223.5 5.0 %all-to-all-done.20 = bf16[16,16,512]{2,1,0:T(8,128)(2,1)} async-done(((bf16[16,16,512]{2,1,0:T(8,128)(2,1)}), bf16[16,16,512]{2,1,0:T(8,128)(2,1)}, u32[]{:S(2)}, u32[]{:S(2)}) %all-to-all-start.20) | async-done | bytes 262176 | tf_op jit(solution)/shard_map/all_to_all | solution.py:138
  253.8 6.0 %all-to-all-done.21 = bf16[2,128,512]{2,0,1:T(2,128)(2,1)S(1)} async-done(((bf16[2,128,512]{2,0,1:T(2,128)(2,1)}), bf16[2,128,512]{2,0,1:T(2,128)(2,1)S(1)}, u32[]{:S(2)}, u32[]{:S(2)}) %all-to-all-start.21) | async-done | bytes 262176 | tf_op jit(solution)/shard_map/all_to_all | solution.py:150
  274.2 6.1 %all-to-all-done.27 = bf16[2,128,512]{2,0,1:T(2,128)(2,1)S(1)} async-done(((bf16[2,128,512]{2,0,1:T(2,128)(2,1)}), bf16[2,128,512]{2,0,1:T(2,128)(2,1)S(1)}, u32[]{:S(2)}, u32[]{:S(2)}) %all-to-all-start.27) | async-done | bytes 262176 | tf_op jit(solution)/shard_map/all_to_all | solution.py:150
  285.2 5.4 %all-to-all-done.28 = bf16[2,128,512]{2,0,1:T(2,128)(2,1)S(1)} async-done(((bf16[2,128,512]{2,0,1:T(2,128)(2,1)}), bf16[2,128,512]{2,0,1:T(2,128)(2,1)S(1)}, u32[]{:S(2)}, u32[]{:S(2)}) %all-to-all-start.28) | async-done | bytes 262176 | tf_op jit(solution)/shard_map/all_to_all | solution.py:151
  303.8 4.6 all-to-all-done.29
  313.5 5.1 %all-to-all-done.30 = bf16[2,128,512]{2,0,1:T(2,128)(2,1)S(1)} async-done(((bf16[2,128,512]{2,0,1:T(2,128)(2,1)}), bf16[2,128,512]{2,0,1:T(2,128)(2,1)S(1)}, u32[]{:S(2)}, u32[]{:S(2)}) %all-to-all-start.30) | async-done | bytes 262176 | tf_op jit(solution)/shard_map/all_to_all | solution.py:152
  322.9 7.6 %all-to-all-done.31 = bf16[2,128,512]{2,0,1:T(2,128)(2,1)S(1)} async-done(((bf16[2,128,512]{2,0,1:T(2,128)(2,1)}), bf16[2,128,512]{2,0,1:T(2,128)(2,1)S(1)}, u32[]{:S(2)}, u32[]{:S(2)}) %all-to-all-start.31) | async-done | bytes 262176 | tf_op jit(solution)/shard_map/all_to_all | solution.py:153
  335.1 7.9 %all-to-all-done.33 = bf16[2,128,512]{2,0,1:T(2,128)(2,1)S(1)} async-done(((bf16[2,128,512]{2,0,1:T(2,128)(2,1)}), bf16[2,128,512]{2,0,1:T(2,128)(2,1)S(1)}, u32[]{:S(2)}, u32[]{:S(2)}) %all-to-all-start.33) | async-done | bytes 262176 | tf_op jit(solution)/shard_map/all_to_all | solution.py:152
  357.0 6.6 %all-to-all-done.6 = bf16[2,128,512]{2,0,1:T(2,128)(2,1)S(1)} async-done(((bf16[2,128,512]{2,0,1:T(2,128)(2,1)}), bf16[2,128,512]{2,0,1:T(2,128)(2,1)S(1)}, u32[]{:S(2)}, u32[]{:S(2)}) %all-to-all-start.6) | async-done | bytes 262176 | tf_op jit(solution)/shard_map/all_to_all | solution.py:148
  369.2 4.6 all-to-all-done.7
  378.3 5.8 %all-to-all-done.15 = bf16[2,128,512]{2,0,1:T(2,128)(2,1)S(1)} async-done(((bf16[2,128,512]{2,0,1:T(2,128)(2,1)}), bf16[2,128,512]{2,0,1:T(2,128)(2,1)S(1)}, u32[]{:S(2)}, u32[]{:S(2)}) %all-to-all-start.15) | async-done | bytes 262176 | tf_op jit(solution)/shard_map/all_to_all | solution.py:148
  387.8 6.6 %all-to-all-done.16 = bf16[2,128,512]{2,0,1:T(2,128)(2,1)S(1)} async-done(((bf16[2,128,512]{2,0,1:T(2,128)(2,1)}), bf16[2,128,512]{2,0,1:T(2,128)(2,1)S(1)}, u32[]{:S(2)}, u32[]{:S(2)}) %all-to-all-start.16) | async-done | bytes 262176 | tf_op jit(solution)/shard_map/all_to_all | solution.py:149
  415.8 5.1 %all-to-all-done.8 = bf16[8,16,512]{2,1,0:T(8,128)(2,1)S(1)} async-done(((bf16[8,16,512]{2,1,0:T(8,128)(2,1)}), bf16[8,16,512]{2,1,0:T(8,128)(2,1)S(1)}, u32[]{:S(2)}, u32[]{:S(2)}) %all-to-all-start.8) | async-done | bytes 131104 | tf_op jit(solution)/shard_map/all_to_all | solution.py:161
  420.9 7.9 %all_to_all.577 = bf16[8,16,512]{2,1,0:T(8,128)(2,1)S(1)} all-to-all(bf16[8,16,512]{2,1,0:T(8,128)(2,1)S(1)} %copy.350), channel_id=1, replica_groups=mesh['seq'=8,'chan'=4] {'seq'}, dimensions={0} | all-to-all | bytes 262144 | tf_op jit(solution)/shard_map/all_to_all | solution.py:161
  434.7 13.1 %all-to-all-done.36 = bf16[128,8,512]{0,2,1:T(8,128)(2,1)S(1)} async-done(((bf16[128,8,512]{0,2,1:T(8,128)(2,1)}), bf16[128,8,512]{0,2,1:T(8,128)(2,1)S(1)}, u32[]{:S(2)}, u32[]{:S(2)}) %all-to-all-start.36) | async-done | bytes 1048608 | tf_op jit(solution)/shard_map/all_to_all | solution.py:180
  (298 shorter events, 288.3 us)
Async XLA Ops:
  11.2 17.2 %all-to-all-start.24 = ((bf16[8,2,4096]{2,1,0:T(2,128)(2,1)}), bf16[8,2,4096]{2,1,0:T(2,128)(2,1)S(1)}, u32[]{:S(2)}, u32[]{:S(2)}) async-start(bf16[8,2,4096]{2,1,0:T(2,128)(2,1)} %reshape.181), calls=%async_computation.24 | async-start | bytes 262144 | tf_op jit(solution)/shard_map/all_to_all | solution.py:127
  80.5 10.4 %all-to-all-start.25 = ((bf16[16,16,512]{2,1,0:T(8,128)(2,1)}), bf16[16,16,512]{2,1,0:T(8,128)(2,1)S(1)}, u32[]{:S(2)}, u32[]{:S(2)}) async-start(bf16[16,16,512]{2,1,0:T(8,128)(2,1)} %copy.372), calls=%async_computation.25 | async-start | bytes 524288 | tf_op jit(solution)/shard_map/all_to_all | solution.py:137
  90.9 12.2 %all-to-all-start.26 = ((bf16[16,16,512]{2,1,0:T(8,128)(2,1)}), bf16[16,16,512]{2,1,0:T(8,128)(2,1)S(1)}, u32[]{:S(2)}, u32[]{:S(2)}) async-start(bf16[16,16,512]{2,1,0:T(8,128)(2,1)} %copy.375), calls=%async_computation.26 | async-start | bytes 524288 | tf_op jit(solution)/shard_map/all_to_all | solution.py:138
  103.1 11.1 %all-to-all-start.13 = ((bf16[16,16,512]{2,1,0:T(8,128)(2,1)}), bf16[16,16,512]{2,1,0:T(8,128)(2,1)S(1)}, u32[]{:S(2)}, u32[]{:S(2)}) async-start(bf16[16,16,512]{2,1,0:T(8,128)(2,1)} %copy.334), calls=%async_computation.13 | async-start | bytes 524288 | tf_op jit(solution)/shard_map/all_to_all | solution.py:135
  124.5 10.3 %all-to-all-start.10 = ((bf16[16,16,512]{2,1,0:T(8,128)(2,1)}), bf16[16,16,512]{2,1,0:T(8,128)(2,1)S(1)}, u32[]{:S(2)}, u32[]{:S(2)}) async-start(bf16[16,16,512]{2,1,0:T(8,128)(2,1)} %copy.325), calls=%async_computation.10 | async-start | bytes 524288 | tf_op jit(solution)/shard_map/all_to_all | solution.py:133
  145.1 30.7 %all-to-all-start.5 = ((bf16[16,16,512]{2,1,0:T(8,128)(2,1)}), bf16[16,16,512]{2,1,0:T(8,128)(2,1)}, u32[]{:S(2)}, u32[]{:S(2)}) async-start(bf16[16,16,512]{2,1,0:T(8,128)(2,1)} %copy.308), calls=%async_computation.5 | async-start | bytes 524288 | tf_op jit(solution)/shard_map/all_to_all | solution.py:136
  175.8 10.9 %all-to-all-start.4 = ((bf16[16,16,512]{2,1,0:T(8,128)(2,1)}), bf16[16,16,512]{2,1,0:T(8,128)(2,1)S(1)}, u32[]{:S(2)}, u32[]{:S(2)}) async-start(bf16[16,16,512]{2,1,0:T(8,128)(2,1)} %copy.305), calls=%async_computation.4 | async-start | bytes 524288 | tf_op jit(solution)/shard_map/all_to_all | solution.py:135
  186.6 10.3 %all-to-all-start.1 = ((bf16[16,16,512]{2,1,0:T(8,128)(2,1)}), bf16[16,16,512]{2,1,0:T(8,128)(2,1)S(1)}, u32[]{:S(2)}, u32[]{:S(2)}) async-start(bf16[16,16,512]{2,1,0:T(8,128)(2,1)} %copy.296), calls=%async_computation.1 | async-start | bytes 524288 | tf_op jit(solution)/shard_map/all_to_all | solution.py:133
  196.9 10.3 %all-to-all-start.2 = ((bf16[16,16,512]{2,1,0:T(8,128)(2,1)}), bf16[16,16,512]{2,1,0:T(8,128)(2,1)S(1)}, u32[]{:S(2)}, u32[]{:S(2)}) async-start(bf16[16,16,512]{2,1,0:T(8,128)(2,1)} %copy.299), calls=%async_computation.2 | async-start | bytes 524288 | tf_op jit(solution)/shard_map/all_to_all | solution.py:134
  207.2 10.3 %all-to-all-start.19 = ((bf16[16,16,512]{2,1,0:T(8,128)(2,1)}), bf16[16,16,512]{2,1,0:T(8,128)(2,1)S(1)}, u32[]{:S(2)}, u32[]{:S(2)}) async-start(bf16[16,16,512]{2,1,0:T(8,128)(2,1)} %copy.354), calls=%async_computation.19 | async-start | bytes 524288 | tf_op jit(solution)/shard_map/all_to_all | solution.py:137
  217.5 11.0 %all-to-all-start.20 = ((bf16[16,16,512]{2,1,0:T(8,128)(2,1)}), bf16[16,16,512]{2,1,0:T(8,128)(2,1)}, u32[]{:S(2)}, u32[]{:S(2)}) async-start(bf16[16,16,512]{2,1,0:T(8,128)(2,1)} %copy.357), calls=%async_computation.20 | async-start | bytes 524288 | tf_op jit(solution)/shard_map/all_to_all | solution.py:138
  259.8 10.3 %all-to-all-start.22 = ((bf16[2,128,512]{2,0,1:T(2,128)(2,1)}), bf16[2,128,512]{2,0,1:T(2,128)(2,1)S(1)}, u32[]{:S(2)}, u32[]{:S(2)}) async-start(bf16[2,128,512]{2,0,1:T(2,128)(2,1)} %copy.365), calls=%async_computation.22 | async-start | bytes 524288 | tf_op jit(solution)/shard_map/all_to_all | solution.py:151
  263.2 165.6 %all-gather.5.cloned.1.call-start = ((), (), s32[]{:S(2)}) async-start(), calls=%async_computation.38 | async-start | bytes 1310720 | tf_op jit(solution)/shard_map/all_gather | solution.py:114
  270.1 10.3 %all-to-all-start.27 = ((bf16[2,128,512]{2,0,1:T(2,128)(2,1)}), bf16[2,128,512]{2,0,1:T(2,128)(2,1)S(1)}, u32[]{:S(2)}, u32[]{:S(2)}) async-start(bf16[2,128,512]{2,0,1:T(2,128)(2,1)} %copy.380), calls=%async_computation.27 | async-start | bytes 524288 | tf_op jit(solution)/shard_map/all_to_all | solution.py:150
  280.4 10.3 %all-to-all-start.28 = ((bf16[2,128,512]{2,0,1:T(2,128)(2,1)}), bf16[2,128,512]{2,0,1:T(2,128)(2,1)S(1)}, u32[]{:S(2)}, u32[]{:S(2)}) async-start(bf16[2,128,512]{2,0,1:T(2,128)(2,1)} %copy.383), calls=%async_computation.28 | async-start | bytes 524288 | tf_op jit(solution)/shard_map/all_to_all | solution.py:151
  308.3 10.3 %all-to-all-start.30 = ((bf16[2,128,512]{2,0,1:T(2,128)(2,1)}), bf16[2,128,512]{2,0,1:T(2,128)(2,1)S(1)}, u32[]{:S(2)}, u32[]{:S(2)}) async-start(bf16[2,128,512]{2,0,1:T(2,128)(2,1)} %copy.387), calls=%async_computation.30 | async-start | bytes 524288 | tf_op jit(solution)/shard_map/all_to_all | solution.py:152
  311.8 136.5 %all-gather.3.cloned.1.call-start = ((), (), s32[]{:S(2)}) async-start(), calls=%async_computation.37 | async-start | bytes 2359296 | tf_op jit(solution)/shard_map/all_gather | solution.py:184
  318.6 11.9 %all-to-all-start.31 = ((bf16[2,128,512]{2,0,1:T(2,128)(2,1)}), bf16[2,128,512]{2,0,1:T(2,128)(2,1)S(1)}, u32[]{:S(2)}, u32[]{:S(2)}) async-start(bf16[2,128,512]{2,0,1:T(2,128)(2,1)} %copy.390), calls=%async_computation.31 | async-start | bytes 524288 | tf_op jit(solution)/shard_map/all_to_all | solution.py:153
  330.6 12.4 %all-to-all-start.33 = ((bf16[2,128,512]{2,0,1:T(2,128)(2,1)}), bf16[2,128,512]{2,0,1:T(2,128)(2,1)S(1)}, u32[]{:S(2)}, u32[]{:S(2)}) async-start(bf16[2,128,512]{2,0,1:T(2,128)(2,1)} %copy.394), calls=%async_computation.33 | async-start | bytes 524288 | tf_op jit(solution)/shard_map/all_to_all | solution.py:152
  353.2 10.3 %all-to-all-start.6 = ((bf16[2,128,512]{2,0,1:T(2,128)(2,1)}), bf16[2,128,512]{2,0,1:T(2,128)(2,1)S(1)}, u32[]{:S(2)}, u32[]{:S(2)}) async-start(bf16[2,128,512]{2,0,1:T(2,128)(2,1)} %copy.315), calls=%async_computation.6 | async-start | bytes 524288 | tf_op jit(solution)/shard_map/all_to_all | solution.py:148
  363.5 10.3 %all-to-all-start.7 = ((bf16[2,128,512]{2,0,1:T(2,128)(2,1)}), bf16[2,128,512]{2,0,1:T(2,128)(2,1)S(1)}, u32[]{:S(2)}, u32[]{:S(2)}) async-start(bf16[2,128,512]{2,0,1:T(2,128)(2,1)} %copy.318), calls=%async_computation.7 | async-start | bytes 524288 | tf_op jit(solution)/shard_map/all_to_all | solution.py:149
  373.8 10.3 %all-to-all-start.15 = ((bf16[2,128,512]{2,0,1:T(2,128)(2,1)}), bf16[2,128,512]{2,0,1:T(2,128)(2,1)S(1)}, u32[]{:S(2)}, u32[]{:S(2)}) async-start(bf16[2,128,512]{2,0,1:T(2,128)(2,1)} %copy.344), calls=%async_computation.15 | async-start | bytes 524288 | tf_op jit(solution)/shard_map/all_to_all | solution.py:148
  384.1 10.3 %all-to-all-start.16 = ((bf16[2,128,512]{2,0,1:T(2,128)(2,1)}), bf16[2,128,512]{2,0,1:T(2,128)(2,1)S(1)}, u32[]{:S(2)}, u32[]{:S(2)}) async-start(bf16[2,128,512]{2,0,1:T(2,128)(2,1)} %copy.347), calls=%async_computation.16 | async-start | bytes 524288 | tf_op jit(solution)/shard_map/all_to_all | solution.py:149
  428.8 18.9 %all-to-all-start.36 = ((bf16[128,8,512]{0,2,1:T(8,128)(2,1)}), bf16[128,8,512]{0,2,1:T(8,128)(2,1)S(1)}, u32[]{:S(2)}, u32[]{:S(2)}) async-start(bf16[128,8,512]{0,2,1:T(8,128)(2,1)} %bitcast.496), calls=%async_computation.36 | async-start | bytes 2097152 | tf_op jit(solution)/shard_map/all_to_all | solution.py:180
  (36 other events, 404.6 us)
Sparse Core Ops, SparseCore 0:
  265.6 29.6 all-gather.4
  315.1 32.2 all-gather.2
where the time goes:
time: 467 us; the launch traced here: 460 us
  waiting for transfers between devices  171 us (37%)
  starting transfers between devices  141 us (30%)
  matrix products  66.8 us (14%)
  local copies, waits for them, and re-layouts  44.9 us (10%)
  between operations  15.8 us (3%)
  other arithmetic  13 us (3%)
  blocking collectives  7.91 us (2%)
    dot_general x72, matrix products, mixed_sum(): return jnp.einsum(form, matrix, operand, precision=FULL_PRECISION)  63.9 us
    all_to_all x2, starting transfers between devices, shards(): lax.all_to_all(turned[3], 'seq', split_axis=0, concat_axis=1, tiled=True)  18.6 us
    all_to_all x1, waiting for transfers between devices, shards(): lax.all_to_all(features, 'seq', split_axis=1, concat_axis=0, tiled=True)  13.1 us
    all_to_all x2, waiting for transfers between devices, shards(): lax.all_to_all(rowed[4], 'seq', split_axis=1, concat_axis=0, tiled=True)  12.9 us
    all_to_all x2, waiting for transfers between devices, shards(): lax.all_to_all(rowed[0], 'seq', split_axis=1, concat_axis=0, tiled=True)  12.4 us
    all_to_all x2, waiting for transfers between devices, shards(): lax.all_to_all(rowed[2], 'seq', split_axis=1, concat_axis=0, tiled=True)  12.1 us
    all_to_all x2, waiting for transfers between devices, shards(): lax.all_to_all(turned[2], 'seq', split_axis=0, concat_axis=1, tiled=True)  11.5 us
    convert_element_type x12, local copies, waits for them, and re-layouts, outer_forward(): return (turned_real.astype(jnp.bfloat16), turned_other.astype(jnp.bfloat16))  11.3 us
  transfers between devices with their start and end apart: 38, of which 33 were waited for; matrix products, arithmetic and copies ran while one was open for 19% of the time, Pallas kernels for 0%

commit v1 on v0

v1 whole, which is shorter than its diff:
```python
import math

import jax
import jax.numpy as jnp
import numpy as np
from jax import lax
from jax.sharding import PartitionSpec as P


def half_shift_table(span):
    step = (2 * np.arange(span)[:, None] + 1) * np.arange(span)[None, :] % (4 * span)
    angle = step * (2.0 * math.pi / (4 * span))
    return np.concatenate([np.cos(angle), -np.sin(angle)], axis=0).astype(jnp.bfloat16)


def product(ar, ai, br, bi):
    return ar * br - ai * bi, ar * bi + ai * br


def against(ar, ai, br, bi):
    return ar * br + ai * bi, ai * br - ar * bi


def phase_products(mixed, taps, gated, span):
    phases = mixed[0].shape[1]
    angle = (np.arange(span) + 0.5) * (math.pi / span)
    turn_cos = jnp.asarray(np.cos(angle), jnp.float32)[:, None]
    turn_sin = jnp.asarray(np.sin(angle), jnp.float32)[:, None]

    def at(pair, phase):
        return pair[0][:, phase], pair[1][:, phase]

    def total(terms):
        return sum(t[0] for t in terms), sum(t[1] for t in terms)

    def convolve(x, h, phase):
        near = [product(*at(x, a), *at(h, phase - a)) for a in range(phase + 1)]
        far = [product(*at(x, a), *at(h, phase - a + phases)) for a in range(phase + 1, phases)]
        out = total(near)
        if far:
            turned = product(*total(far), turn_cos, -turn_sin)
            out = total([out, turned])
        return out

    def correlate(g, h, phase):
        near = [against(*at(g, a), *at(h, a - phase)) for a in range(phase, phases)]
        far = [against(*at(g, a), *at(h, a - phase + phases)) for a in range(phase)]
        out = total(near)
        if far:
            turned = product(*total(far), turn_cos, turn_sin)
            out = total([out, turned])
        return out

    outs = []
    for rule, first, second in ((convolve, mixed, taps), (correlate, gated, taps), (correlate, gated, mixed)):
        parts = [rule(first, second, phase) for phase in range(phases)]
        real = jnp.stack([p[0] for p in parts], axis=1)
        other = jnp.stack([p[1] for p in parts], axis=1)
        outs.append((real, other))
    return outs


def times(first, second):
    return (first.astype(jnp.float32) * second.astype(jnp.float32)).astype(jnp.bfloat16)


def shards(layer_input, gate_query, gate_key, value_proj, grad_out, filter_taps):
    rows, width = gate_query.shape
    blocks = lax.axis_size("seq")
    length = rows * blocks
    share = width // blocks
    span = min(length, width)
    phases = length // span
    scale_root = 1.0 / math.sqrt(length)
    table = jnp.asarray(half_shift_table(span))

    features = lax.all_gather(layer_input, "chan", axis=1, tiled=True)
    mixed = times(gate_key, value_proj)
    gated = times(grad_out, gate_query)

    def cut(array):
        return array.reshape(rows, blocks, share).transpose(1, 0, 2)

    sent = jnp.stack([cut(mixed), cut(filter_taps), cut(gated), cut(gate_key)], axis=1)
    held = lax.all_to_all(sent, "seq", split_axis=0, concat_axis=0, tiled=True)
    whole = held.transpose(1, 0, 2, 3).reshape(4, length, share)
    signals = whole[:3].reshape(3, span, phases * share).transpose(1, 0, 2).reshape(span, -1)
    spectra = lax.dot_general(
        table, signals, (((1,), (0,)), ((), ())), preferred_element_type=jnp.float32
    ).reshape(2, span, 3, phases, share)
    pairs = [(spectra[0, :, s], spectra[1, :, s]) for s in range(3)]
    results = phase_products(*pairs, span)
    stacked = jnp.stack(
        [jnp.stack([r[0] for r in results], 1), jnp.stack([r[1] for r in results], 1)], 0
    ).astype(jnp.bfloat16)
    back = lax.dot_general(
        table,
        stacked.reshape(2 * span, 3 * phases * share),
        (((0,), (0,)), ((), ())),
        preferred_element_type=jnp.float32,
    ).reshape(span, 3, phases * share)
    weights = jnp.asarray([1.0, 1.0, scale_root], jnp.float32) / span
    back = (back * weights[None, :, None]).astype(jnp.bfloat16)
    back = back.transpose(1, 0, 2).reshape(3, length, share)
    value_all = lax.all_gather(times(back[1], whole[3]), "seq", axis=1, tiled=True)
    restored = lax.all_to_all(
        back.reshape(3, blocks, rows, share).transpose(1, 0, 2, 3),
        "seq", split_axis=0, concat_axis=0, tiled=True,
    ).transpose(1, 2, 0, 3).reshape(3, rows, width)
    columns = lax.all_to_all(features, "seq", split_axis=1, concat_axis=0, tiled=True)
    grad_weight = (
        lax.dot_general(
            columns, value_all, (((0,), (0,)), ((), ())), preferred_element_type=jnp.float32
        )
        * scale_root
    )
    return (
        times(grad_out, restored[0]),
        times(restored[1], value_proj),
        times(restored[1], gate_key),
        restored[2],
        grad_weight,
    )


def solution(mesh):
    spec = P("seq", "chan")
    return jax.shard_map(
        shards, mesh=mesh, in_specs=(spec,) * 6, out_specs=(spec,) * 5, check_vma=False
    )
```

time: 467 us -> 123 us (0.26); the launches traced: 460 us -> 123 us
  starting transfers between devices: 141 us -> 12.5 us
  waiting for transfers between devices: 171 us -> 45.7 us
  matrix products: 66.8 us -> 12.5 us
  local copies, waits for them, and re-layouts: 44.9 us -> 34 us
  other arithmetic: 13 us -> 3.47 us
  blocking collectives: 7.91 us -> 0 us
    all_to_all x35 -> x2, starting transfers between devices: 137 us -> 8.72 us  [the longest x1 5.17 us: shards(): held = lax.all_to_all(sent, 'seq', split_axis=0, concat_axis=0, tiled=True)]
    all_to_all x35 -> x2, waiting for transfers between devices: 158 us -> 29.7 us  [the longest x1 15.3 us: shards(): lax.all_to_all(back.reshape(3, blocks, rows, share).transpose(1, 0, 2, 3)...]
    dot_general x73 -> x3, matrix products: 66.8 us -> 12.5 us  [the longest x1 5.66 us: shards(): lax.dot_general(table, signals, (((1,), (0,)), ((), ())), preferred_eleme...]
    convert_element_type x30 -> x0, local copies, waits for them, and re-layouts: 25.4 us -> none  [the longest x12 11.3 us: outer_forward(): return (turned_real.astype(jnp.bfloat16), turned_other.astype(jnp.bfloat16))]
    unnamed x65 -> x42, local copies, waits for them, and re-layouts: 9.77 us -> 18.7 us
    unnamed x6 -> x0, other arithmetic: 8.47 us -> none
    all_to_all x1 -> x0, blocking collectives: 7.91 us -> none  [shards(): lax.all_to_all(conv_block, 'seq', split_axis=0, concat_axis=1, tiled=True)]
    all_to_all x48 -> x1, local copies, waits for them, and re-layouts: 7.98 us -> 0.66 us  [shards(): held = lax.all_to_all(sent, 'seq', split_axis=0, concat_axis=0, tiled=True)]
  transfers between devices with their start and end apart: 38 -> 5, of which waited for: 33 -> 3; matrix products, arithmetic and copies ran while one was open for 19% -> 31% of each run, Pallas kernels for 0% -> 0%
where the time goes in v1:
time: 123 us
  waiting for transfers between devices  45.7 us (37%)
  local copies, waits for them, and re-layouts  34 us (28%)
  between operations  14.4 us (12%)
  starting transfers between devices  12.5 us (10%)
  matrix products  12.5 us (10%)
  other arithmetic  3.47 us (3%)
    unnamed x42, local copies, waits for them, and re-layouts  18.7 us
    all_to_all x1, waiting for transfers between devices, shards(): lax.all_to_all(features, 'seq', split_axis=1, concat_axis=0, tiled=True)  15.9 us
    all_to_all x1, waiting for transfers between devices, shards(): lax.all_to_all(back.reshape(3, blocks, rows, share).transpose(1, 0, 2, 3)...  15.3 us
    all_to_all x1, waiting for transfers between devices, shards(): held = lax.all_to_all(sent, 'seq', split_axis=0, concat_axis=0, tiled=True)  14.4 us
    dot_general x1, matrix products, shards(): lax.dot_general(table, signals, (((1,), (0,)), ((), ())), preferred_eleme...  5.66 us
    all_to_all x1, starting transfers between devices, shards(): held = lax.all_to_all(sent, 'seq', split_axis=0, concat_axis=0, tiled=True)  5.17 us
    reshape x1, local copies, waits for them, and re-layouts, shards(): spectra = lax.dot_general(table, signals, (((1,), (0,)), ((), ())), prefe...  4.25 us
    dot_general x1, matrix products, shards(): lax.dot_general(table, stacked.reshape(2 * span, 3 * phases * share), (((...  4 us
  transfers between devices with their start and end apart: 5, of which 3 were waited for; matrix products, arithmetic and copies ran while one was open for 31% of the time, Pallas kernels for 0%

profile of v1, /device:TPU:0, one launch (start us, length us, event | category | flops | bytes accessed | tf_op | source)
XLA Modules:
  0.0 122.7 jit_solution(7280602151576740326)
XLA Ops:
  7.2 1.2 copy.253
  8.3 1.1 copy.254
  9.5 1.2 copy.252
  10.7 1.2 copy.256
  13.5 5.2 %all-to-all-start = ((bf16[8,4,128,128]{2,3,1,0:T(8,128)(2,1)}), bf16[8,4,128,128]{2,3,1,0:T(8,128)(2,1)S(1)}, u32[]{:S(2)}, u32[]{:S(2)}) async-start(bf16[8,4,128,128]{2,3,1,0:T(8,128)(2,1)} %copy.258), calls=%async_computation | async-start | bytes 2097152 | tf_op jit(solution)/shard_map/all_to_all | solution.py:85
  19.6 14.4 %all-to-all-done = bf16[8,4,128,128]{2,3,1,0:T(8,128)(2,1)S(1)} async-done(((bf16[8,4,128,128]{2,3,1,0:T(8,128)(2,1)}), bf16[8,4,128,128]{2,3,1,0:T(8,128)(2,1)S(1)}, u32[]{:S(2)}, u32[]{:S(2)}) %all-to-all-start) | async-done | bytes 1048608 | tf_op jit(solution)/shard_map/all_to_all | solution.py:85
  35.7 5.7 %fusion.14 = f32[2048,384]{0,1:T(8,128)} fusion(bf16[2048,1024]{1,0:T(8,128)(2,1)} %constant.9.clone, bf16[1024,384]{0,1:T(8,128)(2,1)S(1)} %bitcast.104), kind=kOutput, calls=%fused_computation.33 | convolution fusion | flops 1610612736 | bytes 8126464 | tf_op jit(solution)/shard_map/dot_general | solution.py:88
  41.4 4.3 %reshape.322 = f32[2,1024,3,1,128]{1,0,4,2,3:T(2,128)S(1)} reshape(f32[2048,384]{0,1:T(8,128)} %fusion.14) | data formatting | bytes 6291456 | tf_op jit(solution)/shard_map/reshape | solution.py:90
  45.6 3.7 %fusion.12 = (f32[1,1024,1,1,128]{1,0,4,2,3:T(1,128)}, f32[1,1024,1,1,128]{1,0,4,2,3:T(1,128)}, f32[1,1024,1,1,128]{1,0,4,2,3:T(1,128)}, f32[1,1024,1,1,128]{1,0...) fusion(f32[2,1024,3,1,128]{1,0,4,2,3:T(2,128)S(1)} %reshape.322), kind=kLoop, calls=%fused_computation.31 | loop fusion | bytes 6291456 | tf_op jit(solution)/shard_map/slice | solution.py:91
  49.3 1.3 %copy.282 = f32[1,1024,1,1,128]{4,1,3,2,0:T(8,128)S(1)} copy(f32[1,1024,1,1,128]{1,0,4,2,3:T(1,128)} %get-tuple-element.54) | data formatting | bytes 1048576
  50.7 1.3 %copy.283 = f32[1,1024,1,1,128]{4,1,3,2,0:T(8,128)S(1)} copy(f32[1,1024,1,1,128]{1,0,4,2,3:T(1,128)} %get-tuple-element.50) | data formatting | bytes 1048576
  52.8 1.2 %copy.286 = f32[1,1024,1,1,128]{4,1,3,2,0:T(8,128)S(1)} copy(f32[1,1024,1,1,128]{1,0,4,2,3:T(1,128)} %get-tuple-element.51) | data formatting | bytes 1048576
  54.0 1.1 copy.287
  55.1 1.5 %fusion.6 = (bf16[1024,1,1,128]{3,0,2,1:T(8,128)(2,1)S(1)}, bf16[1024,1,1,128]{3,0,1,2:T(8,128)(2,1)S(1)}, bf16[1024,1,1,128]{3,0,1,2:T(8,128)(2,1)S(1)}, bf16[1...) fusion(f32[1,1024,1,1,128]{4,1,3,2,0:T(8,128)S(1)} %copy.284, ...), kind=kLoop, calls=%fused_computation.24 | loop fusion | flops 3145728 | bytes 4718592 | tf_op jit(solution)/shard_map/sub | solution.py:17
  56.6 1.7 %slice.68 = bf16[1,8,128,128]{3,2,1,0:T(8,128)(2,1)} slice(bf16[4,8,128,128]{3,2,1,0:T(8,128)(2,1)} %bitcast.90), slice={[3:4], [0:8], [0:128], [0:128]} | slice | bytes 524288 | tf_op jit(solution)/shard_map/slice | solution.py:105
  58.6 1.5 %copy.271 = bf16[2,1024,3,1,128]{1,0,4,2,3:T(2,128)(2,1)S(1)} copy(bf16[2,1024,3,1,128]{4,1,2,3,0:T(8,128)(2,1)S(1)} %pad_maximum_fusion) | data formatting | bytes 3145728 | tf_op jit(solution)/shard_map/stack | solution.py:93
  60.5 4.0 %fusion.15 = f32[1024,384]{0,1:T(8,128)S(1)} fusion(bf16[2048,384]{0,1:T(8,128)(2,1)S(1)} %bitcast.96, bf16[2048,1024]{1,0:T(8,128)(2,1)} %constant.9.clone), kind=kOutput, calls=%fused_computation.34 | convolution fusion | flops 1610612736 | bytes 7340032 | tf_op jit(solution)/shard_map/dot_general | solution.py:96
  67.2 1.2 copy.273
  68.3 3.5 %all-to-all-start.1 = ((bf16[8,3,128,128]{2,3,1,0:T(8,128)(2,1)}), bf16[8,3,128,128]{2,3,1,0:T(8,128)(2,1)S(1)}, u32[]{:S(2)}, u32[]{:S(2)}) async-start(bf16[8,3,128,128]{2,3,1,0:T(8,128)(2,1)} %bitcast.30), calls=%async_computation.1 | async-start | bytes 1572864 | tf_op jit(solution)/shard_map/all_to_all | solution.py:106
  71.9 15.3 %all-to-all-done.1 = bf16[8,3,128,128]{2,3,1,0:T(8,128)(2,1)S(1)} async-done(((bf16[8,3,128,128]{2,3,1,0:T(8,128)(2,1)}), bf16[8,3,128,128]{2,3,1,0:T(8,128)(2,1)S(1)}, u32[]{:S(2)}, u32[]{:S(2)}) %all-to-all-start.1) | async-done | bytes 786464 | tf_op jit(solution)/shard_map/all_to_all | solution.py:106
  87.2 3.7 %all-to-all-start.2 = ((bf16[128,8,512]{0,2,1:T(8,128)(2,1)}), bf16[128,8,512]{0,2,1:T(8,128)(2,1)S(1)}, u32[]{:S(2)}, u32[]{:S(2)}) async-start(bf16[128,8,512]{0,2,1:T(8,128)(2,1)} %bitcast.98), calls=%async_computation.2 | async-start | bytes 2097152 | tf_op jit(solution)/shard_map/all_to_all | solution.py:110
  94.7 15.9 %all-to-all-done.2 = bf16[128,8,512]{0,2,1:T(8,128)(2,1)S(1)} async-done(((bf16[128,8,512]{0,2,1:T(8,128)(2,1)}), bf16[128,8,512]{0,2,1:T(8,128)(2,1)S(1)}, u32[]{:S(2)}, u32[]{:S(2)}) %all-to-all-start.2) | async-done | bytes 1048608 | tf_op jit(solution)/shard_map/all_to_all | solution.py:110
  111.1 2.9 %multiply_bitcast_fusion = f32[512,1024]{0,1:T(8,128)S(1)} fusion(bf16[1024,1024]{1,0:T(8,128)(2,1)} %all-gather.3.cloned.1.call-done, bf16[1024,512]{1,0:T(8,128)(2,1)S(1)} %bitcast.99), kind=kOutput, calls=%fused_computation | convolution fusion | flops 1074266112 | bytes 5242880 | tf_op jit(solution)/shard_map/dot_general | solution.py:112
  114.0 1.8 %copy.280 = f32[512,1024]{1,0:T(8,128)} copy(f32[512,1024]{0,1:T(8,128)S(1)} %multiply_bitcast_fusion) | data formatting | bytes 4194304
  (57 shorter events, 12.5 us)
Async XLA Ops:
  7.2 4.8 %copy-start.9 = (bf16[128,1024]{1,0:T(8,128)(2,1)S(1)}, bf16[128,1024]{1,0:T(8,128)(2,1)}, u32[]{:S(2)}) copy-start(bf16[128,1024]{1,0:T(8,128)(2,1)} %param.13) | copy-start | bytes 786436
  9.5 3.0 %copy-start.3 = (bf16[128,1024]{0,1:T(8,128)(2,1)}, bf16[128,1024]{0,1:T(8,128)(2,1)S(1)}, u32[]{:S(2)}) copy-start(bf16[128,1024]{0,1:T(8,128)(2,1)S(1)} %copy.254) | copy-start | bytes 786436
  10.7 1.7 %copy-start.1 = (bf16[128,1024]{0,1:T(8,128)(2,1)}, bf16[128,1024]{0,1:T(8,128)(2,1)S(1)}, u32[]{:S(2)}) copy-start(bf16[128,1024]{0,1:T(8,128)(2,1)S(1)} %copy.252) | copy-start | bytes 786436
  12.4 6.3 %copy-start.10 = (bf16[128,1024]{1,0:T(8,128)(2,1)S(1)}, bf16[128,1024]{1,0:T(8,128)(2,1)}, u32[]{:S(2)}) copy-start(bf16[128,1024]{1,0:T(8,128)(2,1)} %param.8) | copy-start | bytes 786436
  13.5 20.6 %all-to-all-start = ((bf16[8,4,128,128]{2,3,1,0:T(8,128)(2,1)}), bf16[8,4,128,128]{2,3,1,0:T(8,128)(2,1)S(1)}, u32[]{:S(2)}, u32[]{:S(2)}) async-start(bf16[8,4,128,128]{2,3,1,0:T(8,128)(2,1)} %copy.258), calls=%async_computation | async-start | bytes 2097152 | tf_op jit(solution)/shard_map/all_to_all | solution.py:85
  18.7 53.2 %all-gather.5.cloned.1.call-start = ((), (), s32[]{:S(2)}) async-start(), calls=%async_computation.4 | async-start | bytes 1310720 | tf_op jit(solution)/shard_map/all_gather | solution.py:77
  19.6 91.5 %all-gather.3.cloned.1.call-start = ((), (), s32[]{:S(2)}) async-start(), calls=%async_computation.3 | async-start | bytes 2359296 | tf_op jit(solution)/shard_map/all_gather | solution.py:105
  34.7 1.0 copy-start
  49.3 2.6 %copy-start.7 = (f32[1,1024,1,1,128]{1,0,4,2,3:T(1,128)S(1)}, f32[1,1024,1,1,128]{1,0,4,2,3:T(1,128)}, u32[]{:S(2)}) copy-start(f32[1,1024,1,1,128]{1,0,4,2,3:T(1,128)} %get-tuple-element.53) | copy-start | bytes 1572868
  49.3 3.0 %copy-start.6 = (f32[1,1024,1,1,128]{1,0,4,2,3:T(1,128)S(1)}, f32[1,1024,1,1,128]{1,0,4,2,3:T(1,128)}, u32[]{:S(2)}) copy-start(f32[1,1024,1,1,128]{1,0,4,2,3:T(1,128)} %get-tuple-element.52) | copy-start | bytes 1572868
  50.7 3.4 %copy-start.5 = (f32[1,1024,1,1,128]{1,0,4,2,3:T(1,128)S(1)}, f32[1,1024,1,1,128]{1,0,4,2,3:T(1,128)}, u32[]{:S(2)}) copy-start(f32[1,1024,1,1,128]{1,0,4,2,3:T(1,128)} %get-tuple-element.55) | copy-start | bytes 1572868
  64.5 0.7 copy-start.11
  65.2 0.9 copy-start.8
  68.3 18.9 %all-to-all-start.1 = ((bf16[8,3,128,128]{2,3,1,0:T(8,128)(2,1)}), bf16[8,3,128,128]{2,3,1,0:T(8,128)(2,1)S(1)}, u32[]{:S(2)}, u32[]{:S(2)}) async-start(bf16[8,3,128,128]{2,3,1,0:T(8,128)(2,1)} %bitcast.30), calls=%async_computation.1 | async-start | bytes 1572864 | tf_op jit(solution)/shard_map/all_to_all | solution.py:106
  71.9 19.1 %copy-start.4 = (bf16[128,1024]{0,1:T(8,128)(2,1)S(1)}, bf16[128,1024]{0,1:T(8,128)(2,1)}, u32[]{:S(2)}) copy-start(bf16[128,1024]{0,1:T(8,128)(2,1)} %copy-done.3) | copy-start | bytes 786436
  87.2 23.4 %all-to-all-start.2 = ((bf16[128,8,512]{0,2,1:T(8,128)(2,1)}), bf16[128,8,512]{0,2,1:T(8,128)(2,1)S(1)}, u32[]{:S(2)}, u32[]{:S(2)}) async-start(bf16[128,8,512]{0,2,1:T(8,128)(2,1)} %bitcast.98), calls=%async_computation.2 | async-start | bytes 2097152 | tf_op jit(solution)/shard_map/all_to_all | solution.py:110
  90.9 1.9 %copy-start.2 = (bf16[128,1024]{0,1:T(8,128)(2,1)S(1)}, bf16[128,1024]{0,1:T(8,128)(2,1)}, u32[]{:S(2)}) copy-start(bf16[128,1024]{0,1:T(8,128)(2,1)} %copy-done.1) | copy-start | bytes 786436
Sparse Core Ops, SparseCore 0:
  21.6 29.6 all-gather.4
  67.1 40.8 all-gather.2

commit v2 on v1

--- a/solution.py
+++ b/solution.py
@@ -1,9 +1,12 @@
+import functools
 import math
 
 import jax
 import jax.numpy as jnp
 import numpy as np
 from jax import lax
+from jax.experimental import pallas as pl
+from jax.experimental.pallas import tpu as pltpu
 from jax.sharding import PartitionSpec as P
 
 
@@ -123,8 +126,256 @@
     )
 
 
+def fused_kernel(
+    blocks, groups, scale_root,
+    layer, query, key, value, cotangent, taps, forward_hbm, inverse_hbm,
+    out_query, out_key, out_value, out_filter, out_weight,
+    send, recv, feats, columns, columns_t, prods, own_value, res, rest, values, forward, inverse,
+    sig_send, sig_recv, chan_send, chan_recv, col_send, col_recv,
+    res_send, res_recv, val_send, val_recv, fwd_send, fwd_recv, local_sem,
+):
+    rows, width = key.shape
+    share = width // blocks
+    span = rows * blocks
+    held = columns.shape[1]
+    chips = blocks // 2
+    me = lax.axis_index("seq")
+    group = lax.axis_index("chan")
+    chip = me // 2
+    core = me % 2
+    sibling = me + 1 - 2 * core
+
+    def lanes(index, size=share):
+        return pl.ds(pl.multiple_of(index * size, size), size)
+
+    def block_rows(index):
+        return pl.ds(pl.multiple_of(index * rows, rows), rows)
+
+    def remote(source, target, sends, recvs, slot, device):
+        return pltpu.make_async_remote_copy(
+            src_ref=source, dst_ref=target, send_sem=sends.at[slot], recv_sem=recvs.at[slot],
+            device_id=device, device_id_type=pl.DeviceIdType.MESH,
+        )
+
+    barrier = pltpu.get_barrier_semaphore()
+    for d in range(1, blocks):
+        pl.semaphore_signal(barrier, inc=1, device_id={"seq": (me + d) % blocks},
+                            device_id_type=pl.DeviceIdType.MESH)
+    for d in range(1, groups):
+        pl.semaphore_signal(barrier, inc=1, device_id={"chan": (group + d) % groups},
+                            device_id_type=pl.DeviceIdType.MESH)
+    tables = [
+        pltpu.make_async_copy(forward_hbm, forward, local_sem.at[0]),
+        pltpu.make_async_copy(inverse_hbm, inverse, local_sem.at[1]),
+    ]
+    for copy in tables:
+        copy.start()
+    send[0] = times(key[...], value[...])
+    send[1] = taps[...]
+    send[2] = times(cotangent[...], query[...])
+    send[3] = key[...]
+    pl.semaphore_wait(barrier, blocks + groups - 2)
+
+    signals = []
+    for d in range(1, blocks):
+        peer = (me + d) % blocks
+        copy = remote(send.at[:, :, lanes(peer)], recv.at[:, block_rows(me), :],
+                      sig_send, sig_recv, d - 1, {"seq": peer})
+        copy.start()
+        signals.append(copy)
+    gathers = []
+    for d in range(1, groups):
+        copy = remote(layer, feats.at[group], chan_send, chan_recv, d - 1,
+                      {"chan": (group + d) % groups})
+        copy.start()
+        gathers.append(copy)
+    own_signal = pltpu.make_async_copy(
+        send.at[:, :, lanes(me)], recv.at[:, block_rows(me), :], local_sem.at[2])
+    own_signal.start()
+    own_layer = pltpu.make_async_copy(layer, feats.at[group], local_sem.at[3])
+    own_layer.start()
+
+    for copy in tables:
+        copy.wait()
+    own_signal.wait()
+    own_layer.wait()
+    for copy in signals:
+        copy.wait_recv()
+
+    tile = 2 * rows
+
+    def forward_step(index, carry):
+        low = pl.ds(pl.multiple_of(index * tile, tile), tile)
+        high = pl.ds(pl.multiple_of(span + index * tile, tile), tile)
+        operand = jnp.concatenate([recv[0], recv[1], recv[2]], axis=1)
+        real = jnp.dot(forward[low, :], operand, preferred_element_type=jnp.float32)
+        other = jnp.dot(forward[high, :], operand, preferred_element_type=jnp.float32)
+        m, h, g = [(real[:, i * share : (i + 1) * share], other[:, i * share : (i + 1) * share])
+                   for i in range(3)]
+        for i, pair in enumerate((product(*m, *h), against(*g, *h), against(*g, *m))):
+            prods[low, i * share : (i + 1) * share] = pair[0].astype(jnp.bfloat16)
+            prods[high, i * share : (i + 1) * share] = pair[1].astype(jnp.bfloat16)
+        return carry
+
+    lax.fori_loop(0, span // tile, forward_step, 0)
+
+    for copy in gathers:
+        copy.wait_recv()
+
+    def feature_block(index):
+        return feats.at[index * held // width, :,
+                        pl.ds(pl.multiple_of(index * held % width, held), held)]
+
+    sent_columns = []
+    for d in range(1, blocks):
+        peer = (me + d) % blocks
+        copy = remote(feature_block(peer), columns.at[block_rows(me), :],
+                      col_send, col_recv, d - 1, {"seq": peer})
+        copy.start()
+        sent_columns.append(copy)
+    own_columns = pltpu.make_async_copy(
+        feature_block(me), columns.at[block_rows(me), :], local_sem.at[4])
+    own_columns.start()
+
+    def inverse_step(index, carry):
+        part = pl.ds(pl.multiple_of(index * tile, tile), tile)
+        total = jnp.dot(inverse[part, :], prods[...], preferred_element_type=jnp.float32)
+        total = total * (1.0 / span)
+        res[0, part, :] = total[:, :share].astype(jnp.bfloat16)
+        back = total[:, share : 2 * share].astype(jnp.bfloat16)
+        res[1, part, :] = back
+        res[2, part, :] = (total[:, 2 * share :] * scale_root).astype(jnp.bfloat16)
+        own_value[part, :] = times(back, recv[3, part, :])
+        return carry
+
+    lax.fori_loop(0, span // tile, inverse_step, 0)
+
+    sent_values = []
+    for d in range(1, chips):
+        peer = 2 * ((chip + d) % chips) + core
+        copy = remote(own_value, values.at[:, lanes(me)], val_send, val_recv, d - 1, {"seq": peer})
+        copy.start()
+        sent_values.append(copy)
+    copy = remote(own_value, values.at[:, lanes(me)], val_send, val_recv, chips - 1,
+                  {"seq": sibling})
+    copy.start()
+    sent_values.append(copy)
+    results = []
+    for d in range(1, blocks):
+        peer = (me + d) % blocks
+        copy = remote(res.at[:, block_rows(peer), :], rest.at[:, :, lanes(me)],
+                      res_send, res_recv, d - 1, {"seq": peer})
+        copy.start()
+        results.append(copy)
+    own_result = pltpu.make_async_copy(
+        res.at[:, block_rows(me), :], rest.at[:, :, lanes(me)], local_sem.at[5])
+    own_result.start()
+    own_column_value = pltpu.make_async_copy(own_value, values.at[:, lanes(me)], local_sem.at[6])
+    own_column_value.start()
+
+    own_columns.wait()
+    for copy in sent_columns:
+        copy.wait_recv()
+
+    def turn_step(index, carry):
+        part = pl.ds(pl.multiple_of(index * rows, rows), rows)
+        columns_t[:, part] = columns[part, :].T
+        return carry
+
+    lax.fori_loop(0, blocks, turn_step, 0)
+
+    passed_on = []
+    for d in range(1, chips):
+        sent_values[d - 1].wait_recv()
+        origin = 2 * ((chip + chips - d) % chips) + core
+        copy = remote(values.at[:, lanes(origin)], values.at[:, lanes(origin)],
+                      fwd_send, fwd_recv, d - 1, {"seq": sibling})
+        copy.start()
+        passed_on.append(copy)
+
+    own_result.wait()
+    for copy in results:
+        copy.wait_recv()
+    out_query[...] = times(cotangent[...], rest[0])
+    out_key[...] = times(rest[1], value[...])
+    out_value[...] = times(rest[1], key[...])
+    out_filter[...] = rest[2]
+
+    own_column_value.wait()
+    sent_values[chips - 1].wait_recv()
+    for copy in passed_on:
+        copy.wait_recv()
+
+    wide = 2 * share
+
+    def weight_step(index, carry):
+        part = lanes(index, wide)
+        out_weight[:, part] = scale_root * jnp.dot(
+            columns_t[...], values[:, part], preferred_element_type=jnp.float32)
+        return carry
+
+    lax.fori_loop(0, width // wide, weight_step, 0)
+    for copy in signals + gathers + sent_columns + sent_values + results + passed_on:
+        copy.wait_send()
+
+
+def fused(layer_input, gate_query, gate_key, value_proj, grad_out, filter_taps):
+    rows, width = gate_query.shape
+    blocks = lax.axis_size("seq")
+    groups = lax.axis_size("chan")
+    length = rows * blocks
+    share = width // blocks
+    held = width * groups // blocks
+    table = half_shift_table(length)
+    kind = gate_query.dtype
+    vmem = pl.BlockSpec(memory_space=pltpu.VMEM)
+    hbm = pl.BlockSpec(memory_space=pl.ANY)
+    dma = pltpu.SemaphoreType.DMA
+    signal = jax.ShapeDtypeStruct((rows, width), kind)
+    return pl.pallas_call(
+        functools.partial(fused_kernel, blocks, groups, 1.0 / math.sqrt(length)),
+        out_shape=[signal] * 4 + [jax.ShapeDtypeStruct((held, width), jnp.float32)],
+        in_specs=[vmem] * 6 + [hbm] * 2,
+        out_specs=[vmem] * 5,
+        scratch_shapes=[
+            pltpu.VMEM((4, rows, width), kind),
+            pltpu.VMEM((4, length, share), kind),
+            pltpu.VMEM((groups, rows, width), kind),
+            pltpu.VMEM((length, held), kind),
+            pltpu.VMEM((held, length), kind),
+            pltpu.VMEM((2 * length, 3 * share), kind),
+            pltpu.VMEM((length, share), kind),
+            pltpu.VMEM((3, length, share), kind),
+            pltpu.VMEM((3, rows, width), kind),
+            pltpu.VMEM((length, width), kind),
+            pltpu.VMEM((2 * length, length), kind),
+            pltpu.VMEM((length, 2 * length), kind),
+            dma((blocks - 1,)), dma((blocks - 1,)),
+            dma((groups,)), dma((groups,)),
+            dma((blocks - 1,)), dma((blocks - 1,)),
+            dma((blocks - 1,)), dma((blocks - 1,)),
+            dma((blocks // 2,)), dma((blocks // 2,)),
+            dma((blocks // 2,)), dma((blocks // 2,)),
+            dma((8,)),
+        ],
+        compiler_params=pltpu.CompilerParams(
+            collective_id=0, has_side_effects=True, vmem_limit_bytes=48 * 2**20
+        ),
+    )(layer_input, gate_query, gate_key, value_proj, grad_out, filter_taps,
+      jnp.asarray(table), jnp.asarray(np.ascontiguousarray(table.T)))
+
+
+def body(*arrays):
+    rows, width = arrays[1].shape
+    blocks = lax.axis_size("seq")
+    share = width // blocks
+    if share % 128 == 0 and rows % 16 == 0 and blocks % 2 == 0 and rows * blocks <= width:
+        return tuple(fused(*arrays))
+    return shards(*arrays)
+
+
 def solution(mesh):
     spec = P("seq", "chan")
     return jax.shard_map(
-        shards, mesh=mesh, in_specs=(spec,) * 6, out_specs=(spec,) * 5, check_vma=False
+        body, mesh=mesh, in_specs=(spec,) * 6, out_specs=(spec,) * 5, check_vma=False
     )

time: 123 us -> 73 us (0.59)
  the two profiles are of different devices: /device:TPU:0 before, /device:TPU:15 now
where the time goes in v2:
time: 73 us; the launch traced here: 72.7 us
  Pallas kernels  62.2 us (85%)
  local copies, waits for them, and re-layouts  9.82 us (13%)
    pallas_call x1, Pallas kernels, fused(): pl.pallas_call(functools.partial(fused_kernel, blocks, groups, 1.0 / math...  62.2 us
    unnamed x17, local copies, waits for them, and re-layouts  9.82 us

profile of v2, /device:TPU:15, one launch (start us, length us, event | category | flops | bytes accessed | tf_op | source)
XLA Modules:
  0.0 72.7 jit_solution(18352170357530003077)
XLA Ops:
  0.6 0.0 copy-start
  0.6 0.9 %copy-done = bf16[128,1024]{1,0:T(8,128)(2,1)S(1)} copy-done((bf16[128,1024]{1,0:T(8,128)(2,1)S(1)}, bf16[128,1024]{1,0:T(8,128)(2,1)}, u32[]{:S(2)}) %copy-start) | copy-done | bytes 262168
  1.6 0.0 copy-start.1
  1.6 0.9 %copy-done.1 = bf16[128,1024]{1,0:T(8,128)(2,1)S(1)} copy-done((bf16[128,1024]{1,0:T(8,128)(2,1)S(1)}, bf16[128,1024]{1,0:T(8,128)(2,1)}, u32[]{:S(2)}) %copy-start.1) | copy-done | bytes 262168
  2.5 0.0 copy-start.2
  2.5 0.9 %copy-done.2 = bf16[128,1024]{1,0:T(8,128)(2,1)S(1)} copy-done((bf16[128,1024]{1,0:T(8,128)(2,1)S(1)}, bf16[128,1024]{1,0:T(8,128)(2,1)}, u32[]{:S(2)}) %copy-start.2) | copy-done | bytes 262168
  3.5 0.0 copy-start.3
  3.5 0.9 %copy-done.3 = bf16[128,1024]{1,0:T(8,128)(2,1)S(1)} copy-done((bf16[128,1024]{1,0:T(8,128)(2,1)S(1)}, bf16[128,1024]{1,0:T(8,128)(2,1)}, u32[]{:S(2)}) %copy-start.3) | copy-done | bytes 262168
  4.4 0.0 copy-start.4
  4.4 0.9 %copy-done.4 = bf16[128,1024]{1,0:T(8,128)(2,1)S(1)} copy-done((bf16[128,1024]{1,0:T(8,128)(2,1)S(1)}, bf16[128,1024]{1,0:T(8,128)(2,1)}, u32[]{:S(2)}) %copy-start.4) | copy-done | bytes 262168
  5.4 0.0 copy-start.5
  5.4 0.9 %copy-done.5 = bf16[128,1024]{1,0:T(8,128)(2,1)S(1)} copy-done((bf16[128,1024]{1,0:T(8,128)(2,1)S(1)}, bf16[128,1024]{1,0:T(8,128)(2,1)}, u32[]{:S(2)}) %copy-start.5) | copy-done | bytes 262168
  6.3 62.2 %shard_map.119 = (bf16[128,1024]{1,0:T(8,128)(2,1)S(1)}, bf16[128,1024]{1,0:T(8,128)(2,1)S(1)}, bf16[128,1024]{1,0:T(8,128)(2,1)S(1)}, bf16[128,1024]{1,0:T(8,128)(2,1)S(1)}, f32[512,1024]{1,0:T(8,128)S(1)}) custom-call(bf16[128,1024]{1,0:T(8,128)(2,1)S(1)} %copy-done, bf16[128,1024]{1,0:T(8,128)(2,1)S(1)} %copy-done.1, bf16[128,1024]{1,0:T(8,128)(2,1)S(1)} %copy-done.2, ...), custom_call_target="tpu_custom_call" | custom-call | tf_op jit(solution)/shard_map/pallas_call | solution.py:335
  68.5 0.7 copy.18
  69.2 0.7 copy.19
  69.9 0.7 copy.20
  70.6 0.7 copy.21
  71.3 1.3 %copy.22 = f32[512,1024]{1,0:T(8,128)} copy(f32[512,1024]{1,0:T(8,128)S(1)} %get-tuple-element.14) | data formatting | bytes 4194304
Async XLA Ops:
  0.6 1.0 %copy-start = (bf16[128,1024]{1,0:T(8,128)(2,1)S(1)}, bf16[128,1024]{1,0:T(8,128)(2,1)}, u32[]{:S(2)}) copy-start(bf16[128,1024]{1,0:T(8,128)(2,1)} %layer.1) | copy-start | bytes 786436
  1.6 0.9 %copy-start.1 = (bf16[128,1024]{1,0:T(8,128)(2,1)S(1)}, bf16[128,1024]{1,0:T(8,128)(2,1)}, u32[]{:S(2)}) copy-start(bf16[128,1024]{1,0:T(8,128)(2,1)} %query.1) | copy-start | bytes 786436
  2.5 0.9 %copy-start.2 = (bf16[128,1024]{1,0:T(8,128)(2,1)S(1)}, bf16[128,1024]{1,0:T(8,128)(2,1)}, u32[]{:S(2)}) copy-start(bf16[128,1024]{1,0:T(8,128)(2,1)} %key.1) | copy-start | bytes 786436
  3.5 0.9 %copy-start.3 = (bf16[128,1024]{1,0:T(8,128)(2,1)S(1)}, bf16[128,1024]{1,0:T(8,128)(2,1)}, u32[]{:S(2)}) copy-start(bf16[128,1024]{1,0:T(8,128)(2,1)} %value.1) | copy-start | bytes 786436
  4.4 0.9 %copy-start.4 = (bf16[128,1024]{1,0:T(8,128)(2,1)S(1)}, bf16[128,1024]{1,0:T(8,128)(2,1)}, u32[]{:S(2)}) copy-start(bf16[128,1024]{1,0:T(8,128)(2,1)} %cotangent.1) | copy-start | bytes 786436
  5.4 0.9 %copy-start.5 = (bf16[128,1024]{1,0:T(8,128)(2,1)S(1)}, bf16[128,1024]{1,0:T(8,128)(2,1)}, u32[]{:S(2)}) copy-start(bf16[128,1024]{1,0:T(8,128)(2,1)} %taps.1) | copy-start | bytes 786436

commit v3 on v2

--- a/solution.py
+++ b/solution.py
@@ -128,13 +128,14 @@
 
 def fused_kernel(
     blocks, groups, scale_root,
-    layer, query, key, value, cotangent, taps, forward_hbm, inverse_hbm,
+    layer_hbm, query_hbm, key_hbm, value_hbm, cotangent_hbm, taps_hbm, forward_hbm, inverse_hbm,
     out_query, out_key, out_value, out_filter, out_weight,
+    layer, query, key, value, cotangent, taps,
     send, recv, feats, columns, columns_t, prods, own_value, res, rest, values, forward, inverse,
     sig_send, sig_recv, chan_send, chan_recv, col_send, col_recv,
-    res_send, res_recv, val_send, val_recv, fwd_send, fwd_recv, local_sem,
+    res_send, res_recv, val_send, val_recv, fwd_send, fwd_recv, local_sem, in_sem,
 ):
-    rows, width = key.shape
+    rows, width = key_hbm.shape
     share = width // blocks
     span = rows * blocks
     held = columns.shape[1]
@@ -157,6 +158,14 @@
             device_id=device, device_id_type=pl.DeviceIdType.MESH,
         )
 
+    inputs = [
+        pltpu.make_async_copy(source, target, in_sem.at[i])
+        for i, (source, target) in enumerate((
+            (key_hbm, key), (value_hbm, value), (cotangent_hbm, cotangent),
+            (query_hbm, query), (taps_hbm, taps), (layer_hbm, layer)))
+    ]
+    for copy in inputs:
+        copy.start()
     barrier = pltpu.get_barrier_semaphore()
     for d in range(1, blocks):
         pl.semaphore_signal(barrier, inc=1, device_id={"seq": (me + d) % blocks},
@@ -170,6 +179,8 @@
     ]
     for copy in tables:
         copy.start()
+    for copy in inputs:
+        copy.wait()
     send[0] = times(key[...], value[...])
     send[1] = taps[...]
     send[2] = times(cotangent[...], query[...])
@@ -248,18 +259,17 @@
         own_value[part, :] = times(back, recv[3, part, :])
         return carry
 
-    lax.fori_loop(0, span // tile, inverse_step, 0)
-
+    halves = [pl.ds(0, span // 2), pl.ds(span // 2, span // 2)]
+    steps = span // tile // 2
     sent_values = []
-    for d in range(1, chips):
-        peer = 2 * ((chip + d) % chips) + core
-        copy = remote(own_value, values.at[:, lanes(me)], val_send, val_recv, d - 1, {"seq": peer})
-        copy.start()
-        sent_values.append(copy)
-    copy = remote(own_value, values.at[:, lanes(me)], val_send, val_recv, chips - 1,
-                  {"seq": sibling})
-    copy.start()
-    sent_values.append(copy)
+    for half, part in enumerate(halves):
+        lax.fori_loop(half * steps, half * steps + steps, inverse_step, 0)
+        for d in range(1, chips + 1):
+            peer = 2 * ((chip + d) % chips) + core if d < chips else sibling
+            copy = remote(own_value.at[part, :], values.at[part, lanes(me)],
+                          val_send, val_recv, half * chips + d - 1, {"seq": peer})
+            copy.start()
+            sent_values.append(copy)
     results = []
     for d in range(1, blocks):
         peer = (me + d) % blocks
@@ -284,14 +294,31 @@
 
     lax.fori_loop(0, blocks, turn_step, 0)
 
+    wide = 2 * share
+
+    def weigh(index):
+        part = lanes(index, wide)
+        out_weight[:, part] = scale_root * jnp.dot(
+            columns_t[...], values[:, part], preferred_element_type=jnp.float32)
+
     passed_on = []
+    for half, part in enumerate(halves):
+        for d in range(1, chips):
+            sent_values[half * chips + d - 1].wait_recv()
+            block = values.at[part, lanes(2 * ((chip + chips - d) % chips) + core)]
+            copy = remote(block, block, fwd_send, fwd_recv, half * chips + d - 1,
+                          {"seq": sibling})
+            copy.start()
+            passed_on.append(copy)
+
+    own_column_value.wait()
+    for half in range(2):
+        sent_values[half * chips + chips - 1].wait_recv()
+    weigh(chip)
     for d in range(1, chips):
-        sent_values[d - 1].wait_recv()
-        origin = 2 * ((chip + chips - d) % chips) + core
-        copy = remote(values.at[:, lanes(origin)], values.at[:, lanes(origin)],
-                      fwd_send, fwd_recv, d - 1, {"seq": sibling})
-        copy.start()
-        passed_on.append(copy)
+        for half in range(2):
+            passed_on[half * (chips - 1) + d - 1].wait_recv()
+        weigh((chip + chips - d) % chips)
 
     own_result.wait()
     for copy in results:
@@ -300,21 +327,6 @@
     out_key[...] = times(rest[1], value[...])
     out_value[...] = times(rest[1], key[...])
     out_filter[...] = rest[2]
-
-    own_column_value.wait()
-    sent_values[chips - 1].wait_recv()
-    for copy in passed_on:
-        copy.wait_recv()
-
-    wide = 2 * share
-
-    def weight_step(index, carry):
-        part = lanes(index, wide)
-        out_weight[:, part] = scale_root * jnp.dot(
-            columns_t[...], values[:, part], preferred_element_type=jnp.float32)
-        return carry
-
-    lax.fori_loop(0, width // wide, weight_step, 0)
     for copy in signals + gathers + sent_columns + sent_values + results + passed_on:
         copy.wait_send()
 
@@ -329,15 +341,15 @@
     table = half_shift_table(length)
     kind = gate_query.dtype
     vmem = pl.BlockSpec(memory_space=pltpu.VMEM)
-    hbm = pl.BlockSpec(memory_space=pl.ANY)
+    hbm = pl.BlockSpec(memory_space=pltpu.HBM)
     dma = pltpu.SemaphoreType.DMA
     signal = jax.ShapeDtypeStruct((rows, width), kind)
     return pl.pallas_call(
         functools.partial(fused_kernel, blocks, groups, 1.0 / math.sqrt(length)),
         out_shape=[signal] * 4 + [jax.ShapeDtypeStruct((held, width), jnp.float32)],
-        in_specs=[vmem] * 6 + [hbm] * 2,
+        in_specs=[hbm] * 8,
         out_specs=[vmem] * 5,
-        scratch_shapes=[
+        scratch_shapes=[pltpu.VMEM((rows, width), kind)] * 6 + [
             pltpu.VMEM((4, rows, width), kind),
             pltpu.VMEM((4, length, share), kind),
             pltpu.VMEM((groups, rows, width), kind),
@@ -354,12 +366,12 @@
             dma((groups,)), dma((groups,)),
             dma((blocks - 1,)), dma((blocks - 1,)),
             dma((blocks - 1,)), dma((blocks - 1,)),
-            dma((blocks // 2,)), dma((blocks // 2,)),
-            dma((blocks // 2,)), dma((blocks // 2,)),
-            dma((8,)),
+            dma((blocks,)), dma((blocks,)),
+            dma((blocks,)), dma((blocks,)),
+            dma((8,)), dma((6,)),
         ],
         compiler_params=pltpu.CompilerParams(
-            collective_id=0, has_side_effects=True, vmem_limit_bytes=48 * 2**20
+            collective_id=0, has_side_effects=True, vmem_limit_bytes=63 * 2**20
         ),
     )(layer_input, gate_query, gate_key, value_proj, grad_out, filter_taps,
       jnp.asarray(table), jnp.asarray(np.ascontiguousarray(table.T)))

time: 73 us -> 73 us (level)
    unnamed x17 -> x5, local copies, waits for them, and re-layouts: 9.82 us -> 9.83 us
where the time goes in v3:
time: 73 us; the launch traced here: 72.8 us
  Pallas kernels  62.3 us (85%)
  local copies, waits for them, and re-layouts  9.83 us (13%)
    pallas_call x1, Pallas kernels, fused(): pl.pallas_call(functools.partial(fused_kernel, blocks, groups, 1.0 / math...  62.3 us
    unnamed x5, local copies, waits for them, and re-layouts  9.83 us

profile of v3, /device:TPU:15, one launch (start us, length us, event | category | flops | bytes accessed | tf_op | source)
XLA Modules:
  0.0 72.8 jit_solution(2523563504271997515)
XLA Ops:
  0.6 62.3 %shard_map.119 = (bf16[128,1024]{1,0:T(8,128)(2,1)}, bf16[128,1024]{1,0:T(8,128)(2,1)}, bf16[128,1024]{1,0:T(8,128)(2,1)}, bf16[128,1024]{1,0:T(8,128)(2,1)}, f32[512,1024]{1,0:T(8,128)}) custom-call(bf16[128,1024]{1,0:T(8,128)(2,1)} %layer_hbm.1, bf16[128,1024]{1,0:T(8,128)(2,1)} %query_hbm.1, bf16[128,1024]{1,0:T(8,128)(2,1)} %key_hbm.1, ...), custom_call_target="tpu_custom_call" | custom-call | tf_op jit(solution)/shard_map/pallas_call | solution.py:347
  62.9 1.7 %copy.18 = bf16[128,1024]{1,0:T(8,128)(2,1)} copy(bf16[128,1024]{1,0:T(8,128)(2,1)} %get-tuple-element.10) | data formatting | bytes 524288
  64.6 1.7 %copy.19 = bf16[128,1024]{1,0:T(8,128)(2,1)} copy(bf16[128,1024]{1,0:T(8,128)(2,1)} %get-tuple-element.11) | data formatting | bytes 524288
  66.3 1.7 %copy.20 = bf16[128,1024]{1,0:T(8,128)(2,1)} copy(bf16[128,1024]{1,0:T(8,128)(2,1)} %get-tuple-element.12) | data formatting | bytes 524288
  67.9 1.7 %copy.21 = bf16[128,1024]{1,0:T(8,128)(2,1)} copy(bf16[128,1024]{1,0:T(8,128)(2,1)} %get-tuple-element.13) | data formatting | bytes 524288
  69.6 3.2 %copy.22 = f32[512,1024]{1,0:T(8,128)} copy(f32[512,1024]{1,0:T(8,128)} %get-tuple-element.14) | data formatting | bytes 4194304

commit v4 on v3

--- a/solution.py
+++ b/solution.py
@@ -371,9 +371,10 @@
             dma((8,)), dma((6,)),
         ],
         compiler_params=pltpu.CompilerParams(
-            collective_id=0, has_side_effects=True, vmem_limit_bytes=63 * 2**20
+            collective_id=0, has_side_effects=True, vmem_limit_bytes=48 * 2**20
         ),
-    )(layer_input, gate_query, gate_key, value_proj, grad_out, filter_taps,
+    )(*[pltpu.with_memory_space_constraint(x, pltpu.HBM) for x in (
+        layer_input, gate_query, gate_key, value_proj, grad_out, filter_taps)],
       jnp.asarray(table), jnp.asarray(np.ascontiguousarray(table.T)))
 
 

time: 73 us -> 65.5 us (0.90)
  local copies, waits for them, and re-layouts: 9.83 us -> 4.13 us
  Pallas kernels: 62.3 us -> 60.6 us
    unnamed x5, local copies, waits for them, and re-layouts: 9.83 us -> 4.13 us
    pallas_call x1, Pallas kernels: 62.3 us -> 60.6 us  [fused(): pl.pallas_call(functools.partial(fused_kernel, blocks, groups, 1.0 / math...]
where the time goes in v4:
time: 65.5 us; the launch traced here: 65.4 us
  Pallas kernels  60.6 us (93%)
  local copies, waits for them, and re-layouts  4.13 us (6%)
    pallas_call x1, Pallas kernels, fused(): pl.pallas_call(functools.partial(fused_kernel, blocks, groups, 1.0 / math...  60.6 us
    unnamed x5, local copies, waits for them, and re-layouts  4.13 us

profile of v4, /device:TPU:15, one launch (start us, length us, event | category | flops | bytes accessed | tf_op | source)
XLA Modules:
  0.0 65.4 jit_solution(2230601273918439798)
XLA Ops:
  0.6 60.6 %shard_map.119 = (bf16[128,1024]{1,0:T(8,128)(2,1)S(1)}, bf16[128,1024]{1,0:T(8,128)(2,1)S(1)}, bf16[128,1024]{1,0:T(8,128)(2,1)S(1)}, bf16[128,1024]{1,0:T(8,128)(2,1)S(1)}, f32[512,1024]{1,0:T(8,128)S(1)}) custom-call(bf16[128,1024]{1,0:T(8,128)(2,1)} %layer_hbm.1, bf16[128,1024]{1,0:T(8,128)(2,1)} %query_hbm.1, bf16[128,1024]{1,0:T(8,128)(2,1)} %key_hbm.1, ...), custom_call_target="tpu_custom_call" | custom-call | tf_op jit(solution)/shard_map/pallas_call | solution.py:347
  61.2 0.7 %copy.18 = bf16[128,1024]{1,0:T(8,128)(2,1)} copy(bf16[128,1024]{1,0:T(8,128)(2,1)S(1)} %get-tuple-element.10) | data formatting | bytes 524288
  61.9 0.7 %copy.19 = bf16[128,1024]{1,0:T(8,128)(2,1)} copy(bf16[128,1024]{1,0:T(8,128)(2,1)S(1)} %get-tuple-element.11) | data formatting | bytes 524288
  62.7 0.7 %copy.20 = bf16[128,1024]{1,0:T(8,128)(2,1)} copy(bf16[128,1024]{1,0:T(8,128)(2,1)S(1)} %get-tuple-element.12) | data formatting | bytes 524288
  63.4 0.7 %copy.21 = bf16[128,1024]{1,0:T(8,128)(2,1)} copy(bf16[128,1024]{1,0:T(8,128)(2,1)S(1)} %get-tuple-element.13) | data formatting | bytes 524288
  64.1 1.3 %copy.22 = f32[512,1024]{1,0:T(8,128)} copy(f32[512,1024]{1,0:T(8,128)S(1)} %get-tuple-element.14) | data formatting | bytes 4194304
